TPU v7x, 32 devices: a whole 2x2x4 slice. The times are simulated.
32 devices in a mesh: grp: 4 (over y, core), row: 4 (over z), col: 2 (over x).
Axes of the slice: x: 2, y: 2, z: 4, core: 2. Of those that a mesh axis runs over, the one named last changes fastest.
Arguments:
- field: float32 [8, 4, 512, 768], P(None, 'grp', 'row', 'col'), may hold values from -6 to 6
- previous: bfloat16 [8, 4, 512, 768], P(None, 'grp', 'row', 'col'), may hold values from -6 to 6
- kappa: float32 [4, 512, 768], P('grp', 'row', 'col'), may hold values from 0.02 to 0.1
- rates: float32 [8], replicated, may hold values from 0.5 to 1.6
- speeds: float32 [8, 3], replicated, may hold values from -0.5 to 0.5
- basis_x: bfloat16 [512, 128], replicated, may hold values from -0.25 to 0.25
- basis_y: bfloat16 [768, 128], replicated, may hold values from -0.21875 to 0.21875
Outputs:
- advanced: float32 [8, 4, 512, 768], P(None, 'grp', 'row', 'col')
- core: float32 [8, 4, 128, 128], P(None, 'grp')
- gram_x: float32 [512, 128], P('row')
- gram_y: float32 [768, 128], P(('col', 'row'))
All inputs are finite; a program needn't handle non-finite values.
Results may differ from a plain program's by a relative error of at most 0.0029.
Values may be sent and summed in bfloat16 or wider, within the bound.
A program may use at most 64 MiB of HBM per device.

v0:
```python
import math

import jax
import jax.numpy as jnp
from jax import lax
from jax.sharding import PartitionSpec as P


def padded_2(value, sides, width):
    for axis, dim in sides:
        devices, length = (lax.axis_size(axis), value.shape[dim])
        up = [(i, (i + 1) % devices) for i in range(devices - 1)]
        down = [(j, i) for i, j in up]
        last = lax.slice_in_dim(value, length - width, length, axis=dim)
        initial = lax.slice_in_dim(value, 0, width, axis=dim)
        before = lax.ppermute(last, axis, up)
        after = lax.ppermute(initial, axis, down)
        value = jnp.concatenate([before, value, after], axis=dim)
    return value


def on_device(field, previous, kappa, rates, speeds, basis_x, basis_y):
    species, depth, width_x, width_y = field.shape
    rank = basis_x.shape[1]
    row_count = lax.axis_size("row")
    col_count = lax.axis_size("col")
    grp_count = lax.axis_size("grp")
    part_y = width_y // row_count
    grid_x = width_x * row_count
    grid_y = width_y * col_count
    grid_z = depth * grp_count
    padded = padded_2(field, (("grp", 1), ("row", 2), ("col", 3)), 1)
    z_next = padded[:, 2:, 1:-1, 1:-1]
    z_prev = padded[:, :-2, 1:-1, 1:-1]
    x_next = padded[:, 1:-1, 2:, 1:-1]
    x_prev = padded[:, 1:-1, :-2, 1:-1]
    y_next = padded[:, 1:-1, 1:-1, 2:]
    y_prev = padded[:, 1:-1, 1:-1, :-2]
    laplace = z_next + z_prev + x_next + x_prev + y_next + y_prev - 6.0 * field
    speed_z = speeds[:, 0][:, None, None, None]
    speed_x = speeds[:, 1][:, None, None, None]
    speed_y = speeds[:, 2][:, None, None, None]
    transport = (
        speed_z * (z_next - z_prev) + speed_x * (x_next - x_prev) + speed_y * (y_next - y_prev)
    )
    advanced = field + kappa[None] * rates[:, None, None, None] * laplace - 0.5 * transport
    scale_x = math.sqrt(grid_x) / (species * grid_z * grid_y)
    scale_y = math.sqrt(grid_y) / (species * grid_z * rank)
    relaid = lax.all_to_all(previous, "row", split_axis=3, concat_axis=2, tiled=True)
    projected = jnp.einsum(
        "szxy,xr->yszr", relaid, basis_x, preferred_element_type=jnp.float32
    ).astype(jnp.bfloat16)
    local_x = lax.psum_scatter(
        scale_x
        * jnp.einsum("szxy,yszr->xr", relaid, projected, preferred_element_type=jnp.float32),
        "row",
        scatter_dimension=0,
        tiled=True,
    )
    y_start = lax.axis_index("col") * width_y + lax.axis_index("row") * part_y
    rows_y = lax.dynamic_slice_in_dim(basis_y, y_start, part_y, 0)
    core_part = jnp.einsum("yszr,yq->szrq", projected, rows_y, preferred_element_type=jnp.float32)
    core = lax.psum(core_part, ("row", "col"))
    core_low = core.astype(jnp.bfloat16)
    local_y = scale_y * jnp.einsum(
        "yszr,szrq->yq", projected, core_low, preferred_element_type=jnp.float32
    )
    gram_y = lax.psum(local_y, "grp")
    gram_x = lax.psum(local_x, ("grp", "col"))
    return (advanced, core, gram_x, gram_y)


def solution(mesh):
    return jax.shard_map(
        on_device,
        mesh=mesh,
        in_specs=(
            P(None, "grp", "row", "col"),
            P(None, "grp", "row", "col"),
            P("grp", "row", "col"),
            P(),
            P(),
            P(),
            P(),
        ),
        out_specs=(
            P(None, "grp", "row", "col"),
            P(None, "grp", None, None),
            P("row", None),
            P(("col", "row"), None),
        ),
        check_vma=False,
    )
```

profile of v0, /device:TPU:0, one launch (start us, length us, event | category | flops | bytes accessed | tf_op | source)
XLA Modules:
  0.0 179.2 jit_solution(5146560700942507453)
XLA Ops:
  8.0 0.0 copy-start
  8.0 0.0 copy-start.6
  8.0 3.5 %copy.38 = f32[8,1,128,384]{3,0,2,1:T(8,128)} copy(f32[8,1,128,384]{3,2,1,0:T(8,128)} %param.7) | data formatting | bytes 3145728 | tf_op args[0]
  11.6 3.5 %collective-permute-start.1 = (f32[8,1,128,384]{3,0,2,1:T(8,128)}, f32[8,1,128,384]{3,0,2,1:T(8,128)}, u32[]{:S(2)}, u32[]{:S(2)}) collective-permute-start(f32[8,1,128,384]{3,0,2,1:T(8,128)} %copy.38), channel_id=1, source_target_pairs={{0,8},{8,16},{16,24},{1,9},{9,17},{17,25},{2,10},{10,18},{18,26},{... | collective-permute-start | bytes 4718600 | tf_op jit(solution)/shard_map/ppermute | solution.py:16
  15.1 0.0 copy-done.6
  15.1 1.3 copy.39
  16.5 5.7 %all-to-all-start = ((bf16[8,1,128,384]{2,0,1,3:T(8,128)(2,1)}), bf16[8,1,128,384]{2,0,1,3:T(8,128)(2,1)S(1)}, u32[]{:S(2)}, u32[]{:S(2)}) async-start(bf16[8,1,128,384]{2,0,1,3:T(8,128)(2,1)} %copy.39), calls=%async_computation | async-start | bytes 1572864 | tf_op jit(solution)/shard_map/all_to_all | solution.py:49
  22.2 0.0 all-reduce.3.cloned.1.call-start
  22.2 1.3 collective-permute-start
  23.5 19.6 %all-to-all-done = bf16[8,1,128,384]{2,0,1,3:T(8,128)(2,1)S(1)} async-done(((bf16[8,1,128,384]{2,0,1,3:T(8,128)(2,1)}), bf16[8,1,128,384]{2,0,1,3:T(8,128)(2,1)S(1)}, u32[]{:S(2)}, u32[]{:S(2)}) %all-to-all-start) | async-done | bytes 786464 | tf_op jit(solution)/shard_map/all_to_all | solution.py:49
  43.1 0.1 copy.40
  43.2 0.0 copy-start.7
  43.2 0.4 copy.41
  43.6 0.3 reshape.44
  43.9 0.2 copy-done.7
  44.1 0.4 fusion.15
  44.4 0.0 copy-start.3
  44.5 0.0 copy-done
  44.5 1.1 convolution_bitcast_fusion
  45.5 0.0 all-reduce.3.cloned.1.call-update
  45.6 0.0 copy-start.2
  45.6 0.0 reduce-scatter.2.cloned.1.call-start
  45.6 0.0 collective-permute-done.1
  45.6 1.6 constant_dynamic-update-slice_fusion.2
  47.2 0.2 copy-done.2
  47.4 0.9 constant_dynamic-update-slice_fusion.1
  48.4 0.0 copy-start.8
  48.4 0.0 collective-permute-done
  48.4 1.6 constant_dynamic-update-slice_fusion
  50.0 0.0 copy-start.1
  50.0 1.3 collective-permute-start.2
  51.3 4.5 %collective-permute-start.3 = (f32[8,3,1,384]{3,0,2,1:T(8,128)S(1)}, f32[8,3,1,384]{3,0,2,1:T(8,128)S(1)}, u32[]{:S(2)}, u32[]{:S(2)}) collective-permute-start(f32[8,3,1,384]{3,0,2,1:T(8,128)S(1)} %get-tuple-element.22), channel_id=1, source_target_pairs={{0,2},{2,4},{4,6},{1,3},{3,5},{5,7},{8,10},{10,12},{12,14},{9,11},... | collective-permute-start | bytes 110600 | tf_op jit(solution)/shard_map/ppermute | solution.py:16
  55.9 0.0 copy-done.8
  55.9 0.2 collective-permute-done.2
  56.0 1.5 collective-permute-done.3
  57.5 2.2 %pad_maximum_fusion.2 = (f32[8,3,130,1]{3,0,2,1:T(8,128)}, f32[8,3,130,1]{3,0,2,1:T(8,128)}) fusion(f32[8,3,1,384]{3,0,2,1:T(8,128)S(1)} %collective-permute-done.2, f32[8,3,128,384]{3,0,2,1:T(8,128)S(1)} %constant_dynamic-update-slice_fusion, f32[8,3,1,384]{3,0,2,1:T(8,128)S(1)} %collective-permute-done.3), kind=kLoop, calls=%fused_computation.2 | loop fusion | flops 12480 | bytes 4817280 | tf_op jit(solution)/shard_map/slice | solution.py:15
  59.7 0.0 copy-done.1
  59.7 2.4 %copy.33 = f32[8,3,130,1]{2,0,3,1:T(8,128)S(1)} copy(f32[8,3,130,1]{3,0,2,1:T(8,128)} %get-tuple-element.20) | data formatting | bytes 24960 | tf_op jit(solution)/shard_map/slice | solution.py:15
  62.1 1.3 collective-permute-start.4
  63.4 2.4 %copy.35 = f32[8,3,130,1]{2,0,3,1:T(8,128)S(1)} copy(f32[8,3,130,1]{3,0,2,1:T(8,128)} %get-tuple-element.21) | data formatting | bytes 24960 | tf_op jit(solution)/shard_map/slice | solution.py:14
  65.8 4.5 %collective-permute-start.5 = (f32[8,3,130,1]{2,0,3,1:T(8,128)S(1)}, f32[8,3,130,1]{2,0,3,1:T(8,128)S(1)}, u32[]{:S(2)}, u32[]{:S(2)}) collective-permute-start(f32[8,3,130,1]{2,0,3,1:T(8,128)S(1)} %copy.35), channel_id=1, source_target_pairs={{0,1},{2,3},{4,5},{6,7},{8,9},{10,11},{12,13},{14,15},{16,17},{18,... | collective-permute-start | bytes 37448 | tf_op jit(solution)/shard_map/ppermute | solution.py:16
  70.3 0.0 copy-done.3
  70.3 1.0 fusion.1
  71.4 0.0 reduce-scatter.2.cloned.1.call-update
  71.4 0.0 copy-start.9
  71.4 0.0 all-reduce.5.cloned.1.call-start
  71.4 0.0 collective-permute-done.4
  71.5 1.0 copy.34
  72.5 0.0 collective-permute-done.5
  72.5 2.1 %copy.36 = f32[8,3,130,1]{3,0,2,1:T(8,128)} copy(f32[8,3,130,1]{2,0,3,1:T(8,128)S(1)} %collective-permute-done.5) | data formatting | bytes 24960 | tf_op jit(solution)/shard_map/ppermute | solution.py:16
  74.6 0.0 copy-done.9
  74.6 8.3 %multiply_subtract_fusion = f32[8,1,128,384]{3,0,2,1:T(8,128)S(1)} fusion(f32[8,1,128,384]{3,0,2,1:T(8,128)} %collective-permute-done, f32[8,1,128,384]{3,0,2,1:T(8,128)} %collective-permute-done.1, f32[8,3,1,384]{3,0,2,1:T(8,128)S(1)} %collective-permute-done.2, f32[8,3,128,384]{3,0,2,1:T(8,128)} %copy-done.1, ...), kind=kLoop, calls=%fused_computation.11 | loop fusion | flops 11010048 | bytes 11305472 | tf_op jit(solution)/shard_map/sub | solution.py:46
  82.9 0.0 copy-start.4
  82.9 1.4 copy.42
  84.4 32.1 %all-reduce.3.cloned.1.call-done = f32[8,1,128,128]{3,2,0,1:T(8,128)} async-done(((f32[8,1,128,128]{3,2,0,1:T(8,128)}), f32[8,1,128,128]{3,2,0,1:T(8,128)}) %all-reduce.3.cloned.1.call-update) | async-done | bytes 524304 | tf_op jit(solution)/shard_map/psum | solution.py:63
  116.5 0.0 copy-done.4
  116.5 1.3 fusion.2
  117.8 0.0 reduce-scatter.2.cloned.1.call-done
  117.9 0.0 all-reduce.5.cloned.1.call-update
  117.9 11.1 %psum.23 = f32[96,128]{1,0:T(8,128)} all-reduce(f32[96,128]{1,0:T(8,128)S(1)} %fusion.2), channel_id=1, replica_groups=mesh['grp'=4,'row'=4,'col'=2] {'grp'}, use_global_device_ids=true, to_apply=%region_3.0 | all-reduce | flops 12288 | bytes 98304 | tf_op jit(solution)/shard_map/psum | solution.py:68
  129.0 40.4 %all-reduce.5.cloned.1.call-done = f32[128,128]{0,1:T(8,128)} async-done(((f32[128,128]{0,1:T(8,128)}), f32[128,128]{0,1:T(8,128)}) %all-reduce.5.cloned.1.call-update) | async-done | bytes 65552 | tf_op jit(solution)/shard_map/psum | solution.py:69
  169.4 1.6 copy.44
  170.9 0.0 copy-done.5
  170.9 0.8 copy.51
  (3 shorter events, 0.0 us)
Async XLA Ops:
  8.0 36.5 %copy-start = (bf16[768,128]{1,0:T(8,128)(2,1)S(1)}, bf16[768,128]{1,0:T(8,128)(2,1)}, u32[]{:S(2)}) copy-start(bf16[768,128]{1,0:T(8,128)(2,1)} %param.13) | copy-start | bytes 589828
  8.0 7.1 %copy-start.6 = (bf16[8,1,128,384]{3,2,1,0:T(8,128)(2,1)S(1)}, bf16[8,1,128,384]{3,2,1,0:T(8,128)(2,1)}, u32[]{:S(2)}) copy-start(bf16[8,1,128,384]{3,2,1,0:T(8,128)(2,1)} %param.8) | copy-start | bytes 2359300
  11.6 34.0 %collective-permute-start.1 = (f32[8,1,128,384]{3,0,2,1:T(8,128)}, f32[8,1,128,384]{3,0,2,1:T(8,128)}, u32[]{:S(2)}, u32[]{:S(2)}) collective-permute-start(f32[8,1,128,384]{3,0,2,1:T(8,128)} %copy.38), channel_id=1, source_target_pairs={{0,8},{8,16},{16,24},{1,9},{9,17},{17,25},{2,10},{10,18},{18,26},{... | collective-permute-start | bytes 4718600 | tf_op jit(solution)/shard_map/ppermute | solution.py:16
  16.5 26.6 %all-to-all-start = ((bf16[8,1,128,384]{2,0,1,3:T(8,128)(2,1)}), bf16[8,1,128,384]{2,0,1,3:T(8,128)(2,1)S(1)}, u32[]{:S(2)}, u32[]{:S(2)}) async-start(bf16[8,1,128,384]{2,0,1,3:T(8,128)(2,1)} %copy.39), calls=%async_computation | async-start | bytes 1572864 | tf_op jit(solution)/shard_map/all_to_all | solution.py:49
  22.2 94.3 %all-reduce.3.cloned.1.call-start = ((), (), s32[]{:S(2)}) async-start(), calls=%async_computation.2 | async-start | bytes 1048576 | tf_op jit(solution)/shard_map/psum | solution.py:63
  22.2 26.2 %collective-permute-start = (f32[8,1,128,384]{3,0,2,1:T(8,128)}, f32[8,1,128,384]{3,0,2,1:T(8,128)}, u32[]{:S(2)}, u32[]{:S(2)}) collective-permute-start(f32[8,1,128,384]{3,0,2,1:T(8,128)} %copy.38), channel_id=1, source_target_pairs={{8,0},{16,8},{24,16},{9,1},{17,9},{25,17},{10,2},{18,10},{26,18},{... | collective-permute-start | bytes 4718600 | tf_op jit(solution)/shard_map/ppermute | solution.py:17
  43.2 0.9 copy-start.7
  44.4 25.9 %copy-start.3 = (f32[128,768]{0,1}, f32[128,768]{0,1:S(1)}, u32[]{:S(2)}) copy-start(f32[128,768]{0,1:S(1)} %fusion.15) | copy-start | bytes 1179652
  45.6 1.9 %copy-start.2 = (f32[8,1,128,384]{3,2,1,0:T(8,128)S(1)}, f32[8,1,128,384]{3,2,1,0:T(8,128)}, u32[]{:S(2)}) copy-start(f32[8,1,128,384]{3,2,1,0:T(8,128)} %param.7) | copy-start | bytes 4718596
  45.6 72.3 %reduce-scatter.2.cloned.1.call-start = ((), (), s32[]{:S(2)}) async-start(), calls=%async_computation.3 | async-start | bytes 327680 | tf_op jit(solution)/shard_map/reduce_scatter | solution.py:53
  48.4 7.5 %copy-start.8 = (f32[8,3]{0,1:T(4,128)S(1)}, f32[8,3]{0,1:T(4,128)}, u32[]{:S(2)}) copy-start(f32[8,3]{0,1:T(4,128)} %param.11) | copy-start | bytes 292
  50.0 9.7 %copy-start.1 = (f32[8,3,128,384]{3,0,2,1:T(8,128)}, f32[8,3,128,384]{3,0,2,1:T(8,128)S(1)}, u32[]{:S(2)}) copy-start(f32[8,3,128,384]{3,0,2,1:T(8,128)S(1)} %constant_dynamic-update-slice_fusion) | copy-start | bytes 14155780
  50.0 6.0 %collective-permute-start.2 = (f32[8,3,1,384]{3,0,2,1:T(8,128)S(1)}, f32[8,3,1,384]{3,0,2,1:T(8,128)S(1)}, u32[]{:S(2)}, u32[]{:S(2)}) collective-permute-start(f32[8,3,1,384]{3,0,2,1:T(8,128)S(1)} %get-tuple-element.23), channel_id=1, source_target_pairs={{2,0},{4,2},{6,4},{3,1},{5,3},{7,5},{10,8},{12,10},{14,12},{11,9},... | collective-permute-start | bytes 110600 | tf_op jit(solution)/shard_map/ppermute | solution.py:17
  51.3 6.2 %collective-permute-start.3 = (f32[8,3,1,384]{3,0,2,1:T(8,128)S(1)}, f32[8,3,1,384]{3,0,2,1:T(8,128)S(1)}, u32[]{:S(2)}, u32[]{:S(2)}) collective-permute-start(f32[8,3,1,384]{3,0,2,1:T(8,128)S(1)} %get-tuple-element.22), channel_id=1, source_target_pairs={{0,2},{2,4},{4,6},{1,3},{3,5},{5,7},{8,10},{10,12},{12,14},{9,11},... | collective-permute-start | bytes 110600 | tf_op jit(solution)/shard_map/ppermute | solution.py:16
  62.1 9.4 %collective-permute-start.4 = (f32[8,3,130,1]{2,0,3,1:T(8,128)S(1)}, f32[8,3,130,1]{2,0,3,1:T(8,128)S(1)}, u32[]{:S(2)}, u32[]{:S(2)}) collective-permute-start(f32[8,3,130,1]{2,0,3,1:T(8,128)S(1)} %copy.33), channel_id=1, source_target_pairs={{1,0},{3,2},{5,4},{7,6},{9,8},{11,10},{13,12},{15,14},{17,16},{19,... | collective-permute-start | bytes 37448 | tf_op jit(solution)/shard_map/ppermute | solution.py:17
  65.8 6.7 %collective-permute-start.5 = (f32[8,3,130,1]{2,0,3,1:T(8,128)S(1)}, f32[8,3,130,1]{2,0,3,1:T(8,128)S(1)}, u32[]{:S(2)}, u32[]{:S(2)}) collective-permute-start(f32[8,3,130,1]{2,0,3,1:T(8,128)S(1)} %copy.35), channel_id=1, source_target_pairs={{0,1},{2,3},{4,5},{6,7},{8,9},{10,11},{12,13},{14,15},{16,17},{18,... | collective-permute-start | bytes 37448 | tf_op jit(solution)/shard_map/ppermute | solution.py:16
  71.4 3.2 %copy-start.9 = (f32[8]{0:T(128)S(1)}, f32[8]{0:T(128)}, u32[]{:S(2)}) copy-start(f32[8]{0:T(128)} %param.10) | copy-start | bytes 100
  71.4 98.0 %all-reduce.5.cloned.1.call-start = ((), (), s32[]{:S(2)}) async-start(), calls=%async_computation.4 | async-start | bytes 131072 | tf_op jit(solution)/shard_map/psum | solution.py:69
  82.9 33.6 %copy-start.4 = (f32[128,768]{0,1:S(1)}, f32[128,768]{0,1}, u32[]{:S(2)}) copy-start(f32[128,768]{0,1} %copy-done.3) | copy-start | bytes 1179652
  116.5 54.4 %copy-start.5 = (f32[8,1,128,128]{3,2,0,1:T(8,128)S(1)}, f32[8,1,128,128]{3,2,0,1:T(8,128)}, u32[]{:S(2)}) copy-start(f32[8,1,128,128]{3,2,0,1:T(8,128)} %all-reduce.3.cloned.1.call-done) | copy-start | bytes 1572868
Sparse Core Ops, SparseCore 0:
  45.7 70.7 all-reduce.2
Sparse Core Ops, SparseCore 1:
  71.5 17.8 reduce-scatter.1
  118.0 51.4 all-reduce.4
where the time goes:
time: 180 us; the launch traced here: 179 us
  waiting for transfers between devices  93.9 us (52%)
  starting transfers between devices  22.3 us (12%)
  local copies, waits for them, and re-layouts  21.9 us (12%)
  between operations  15.7 us (9%)
  blocking collectives  11.1 us (6%)
  other arithmetic  10.5 us (6%)
  matrix products  3.78 us (2%)
    psum x1, waiting for transfers between devices, on_device(): gram_x = lax.psum(local_x, ('grp', 'col'))  40.4 us
    psum x1, waiting for transfers between devices, on_device(): core = lax.psum(core_part, ('row', 'col'))  32.1 us
    all_to_all x1, waiting for transfers between devices, on_device(): lax.all_to_all(previous, 'row', split_axis=3, concat_axis=2, tiled=True)  19.6 us
    ppermute x3, starting transfers between devices, padded_2(): before = lax.ppermute(last, axis, up)  12.6 us
    unnamed x27, local copies, waits for them, and re-layouts  11.6 us
    psum x1, blocking collectives, on_device(): gram_y = lax.psum(local_y, 'grp')  11.1 us
    sub x1, other arithmetic, on_device(): field + kappa[None] * rates[:, None, None, None] * laplace - 0.5 * transport  8.32 us
    all_to_all x1, starting transfers between devices, on_device(): lax.all_to_all(previous, 'row', split_axis=3, concat_axis=2, tiled=True)  5.7 us
  transfers between devices with their start and end apart: 10, of which 5 were waited for; matrix products, arithmetic and copies ran while one was open for 17% of the time, Pallas kernels for 0%

commit v1 on v0

v1 whole, which is shorter than its diff:
```python
import functools
import math

import jax
import jax.numpy as jnp
from jax import lax
from jax.experimental import pallas as pl
from jax.experimental.pallas import tpu as pltpu
from jax.sharding import PartitionSpec as P

MESH = pl.DeviceIdType.MESH


def remote(src, dst, send, recv, target):
    return pltpu.make_async_remote_copy(
        src_ref=src,
        dst_ref=dst,
        send_sem=send,
        recv_sem=recv,
        device_id=target,
        device_id_type=MESH,
    )


def kernel(
    grp_n, row_n, col_n, scale_x, scale_y,
    field, prev, kappa, rates, speeds, basis_x, basis_y,
    advanced, core, gram_x, gram_y,
    field_v, kappa_v, bx_v, by_v, pair_v, q_v, proj_v, part_v, core_v,
    gx_acc, gx_in, gx_piece, gx_all, gy_acc, gy_in, gx_out, gy_out,
    z_out, z_in, x_out, x_in, y_out, y_in, adv_v,
    in_sem, own_sem, pair_s, pair_r, q_s, q_r, part_s, part_r, core_s, core_r, core_l,
    gx1_s, gx1_r, gx2_s, gx2_r, gy_s, gy_r, z_s, z_r, x_s, x_r, y_s, y_r, out_sem, fin_sem,
):
    species, width_x, width_y = field_v.shape
    half = species // 2
    pairs = row_n // 2
    rank = bx_v.shape[1]
    piece = width_x // grp_n
    part_y = width_y // row_n
    g = lax.axis_index("grp")
    r = lax.axis_index("row")
    c = lax.axis_index("col")
    a = r // 2
    b = r % 2
    team = 2 * grp_n
    ring = grp_n * col_n
    me_team = b * grp_n + g
    me_ring = c * grp_n + g

    def team_at(k):
        j = (me_team + k) % team
        return j, j // grp_n, j % grp_n

    def ring_at(k):
        j = (me_ring + k) % ring
        return j, j // grp_n, j % grp_n

    mine = [
        pltpu.make_async_copy(
            prev.at[b * half + i, 0],
            pair_v.at[i, pl.ds(pl.multiple_of(b * width_x, width_x), width_x)],
            own_sem.at[i],
        )
        for i in range(half)
    ]
    loads = [
        pltpu.make_async_copy(field.at[:, 0], field_v, in_sem.at[0]),
        pltpu.make_async_copy(kappa.at[0], kappa_v, in_sem.at[1]),
        pltpu.make_async_copy(
            basis_x.at[pl.ds(pl.multiple_of(a * 2 * width_x, 2 * width_x), 2 * width_x)],
            bx_v, in_sem.at[2],
        ),
        pltpu.make_async_copy(
            basis_y.at[pl.ds(pl.multiple_of(c * width_y, width_y), width_y)], by_v, in_sem.at[3]
        ),
    ]
    loads[0].start()
    for copy in mine:
        copy.start()
    for copy in loads[1:]:
        copy.start()

    barrier = pltpu.get_barrier_semaphore()
    count = 0
    for k in range(1, team):
        _, b_to, g_to = team_at(k)
        pl.semaphore_signal(
            barrier, inc=1, device_id={"grp": g_to, "row": 2 * a + b_to}, device_id_type=MESH
        )
        count += 1
    for d in range(1, col_n):
        for e in range(grp_n):
            pl.semaphore_signal(
                barrier, inc=1,
                device_id={"grp": (g + e) % grp_n, "col": (c + d) % col_n},
                device_id_type=MESH,
            )
            count += 1
    for d in range(1, pairs):
        pl.semaphore_signal(
            barrier, inc=1, device_id={"row": 2 * ((a + d) % pairs) + b}, device_id_type=MESH
        )
        count += 1

    @pl.when(r > 0)
    def _():
        pl.semaphore_signal(barrier, inc=1, device_id={"row": r - 1}, device_id_type=MESH)

    @pl.when(r < row_n - 1)
    def _():
        pl.semaphore_signal(barrier, inc=1, device_id={"row": r + 1}, device_id_type=MESH)

    neighbours = (r + row_n - 1) // row_n + (2 * row_n - 2 - r) // row_n
    pl.semaphore_wait(barrier, count + neighbours)

    def pair_copy(i, sender):
        return remote(
            prev.at[(1 - b) * half + i, 0],
            pair_v.at[i, pl.ds(pl.multiple_of(sender * width_x, width_x), width_x)],
            pair_s.at[i], pair_r.at[i], {"row": 2 * a + 1 - b},
        )

    for i in range(half):
        pair_copy(i, b).start()

    loads[0].wait()
    z_out[...] = field_v[...].astype(jnp.bfloat16)
    sides = (
        ("grp", g, grp_n, z_out, z_in, z_s, z_r),
        ("row", r, row_n, x_out, x_in, x_s, x_r),
        ("col", c, col_n, y_out, y_in, y_s, y_r),
    )

    def halo(axis, at, out, into, send, recv, up, shared):
        slot = 0 if up else 1
        return remote(
            out if shared else out.at[slot], into.at[slot], send.at[slot], recv.at[slot],
            {axis: at + 1 if up else at - 1},
        )

    def send_halos(k):
        axis, at, n, out, into, send, recv = sides[k]

        @pl.when(at < n - 1)
        def _():
            halo(axis, at, out, into, send, recv, True, k == 0).start()

        @pl.when(at > 0)
        def _():
            halo(axis, at, out, into, send, recv, False, k == 0).start()

    send_halos(0)
    lane = lax.broadcasted_iota(jnp.int32, (width_x, 128), 1)
    first = jnp.zeros((width_x, 128), jnp.float32)
    last = jnp.zeros((width_x, 128), jnp.float32)
    for s in range(species):
        x_out[0, s : s + 1, :] = field_v[s, width_x - 1 : width_x, :]
        x_out[1, s : s + 1, :] = field_v[s, 0:1, :]
        last = jnp.where(lane == s, field_v[s, :, width_y - 1 : width_y], last)
        first = jnp.where(lane == s, field_v[s, :, 0:1], first)
    y_out[0] = last
    y_out[1] = first
    send_halos(1)
    send_halos(2)

    def q_copy(i, d, sender, target):
        return remote(
            q_v.at[sender, i], q_v.at[sender, i], q_s.at[d, i], q_r.at[d, i],
            {"row": 2 * target + b},
        )

    loads[2].wait()
    for i in range(half):
        mine[i].wait()
        pair_copy(i, 1 - b).wait_recv()
        q_v[a, i] = lax.dot_general(
            bx_v[...], pair_v[i], (((0,), (0,)), ((), ())), preferred_element_type=jnp.float32
        ).astype(jnp.bfloat16)
        for d in range(1, pairs):
            q_copy(i, d, a, (a + d) % pairs).start()

    loads[1].wait()

    def receive_halos(k):
        axis, at, n, out, into, send, recv = sides[k]

        @pl.when(at > 0)
        def _():
            remote(
                out if k == 0 else out.at[0], into.at[0], send.at[0], recv.at[0], {axis: at - 1}
            ).wait_recv()

        @pl.when(at == 0)
        def _():
            into[0] = jnp.zeros(into.shape[1:], into.dtype)

        @pl.when(at < n - 1)
        def _():
            remote(
                out if k == 0 else out.at[1], into.at[1], send.at[1], recv.at[1], {axis: at + 1}
            ).wait_recv()

        @pl.when(at == n - 1)
        def _():
            into[1] = jnp.zeros(into.shape[1:], into.dtype)

    for k in (2, 1, 0):
        receive_halos(k)
    at_x = lax.broadcasted_iota(jnp.int32, (width_x, width_y), 0)
    at_y = lax.broadcasted_iota(jnp.int32, (width_x, width_y), 1)
    writes = []
    for s in range(species):
        u = field_v[s]
        z_prev = z_in[0, s].astype(jnp.float32)
        z_next = z_in[1, s].astype(jnp.float32)
        x_prev = jnp.where(at_x == 0, x_in[0, s : s + 1, :], pltpu.roll(u, 1, 0))
        x_next = jnp.where(at_x == width_x - 1, x_in[1, s : s + 1, :], pltpu.roll(u, width_x - 1, 0))
        y_prev = jnp.where(at_y == 0, y_in[0, :, s : s + 1], pltpu.roll(u, 1, 1))
        y_next = jnp.where(
            at_y == width_y - 1, y_in[1, :, s : s + 1], pltpu.roll(u, width_y - 1, 1)
        )
        laplace = z_next + z_prev + x_next + x_prev + y_next + y_prev - 6.0 * u
        transport = (
            speeds[s, 0] * (z_next - z_prev)
            + speeds[s, 1] * (x_next - x_prev)
            + speeds[s, 2] * (y_next - y_prev)
        )
        adv_v[s] = u + kappa_v[...] * rates[s] * laplace - 0.5 * transport
        copy = pltpu.make_async_copy(adv_v.at[s], advanced.at[s, 0], out_sem.at[s])
        copy.start()
        writes.append(copy)

    def part_copy(i, d, sender, target):
        return remote(
            part_v.at[sender, i], part_v.at[sender, i], part_s.at[d, i], part_r.at[d, i],
            {"col": target},
        )

    loads[3].wait()
    for i in range(half):
        for d in range(1, pairs):
            sender = (a + pairs - d) % pairs
            q_copy(i, d, sender, sender).wait_recv()
        total = q_v[0, i].astype(jnp.float32)
        for j in range(1, pairs):
            total = total + q_v[j, i].astype(jnp.float32)
        low = total.astype(jnp.bfloat16)
        proj_v[i] = low
        part_v[c, i] = jnp.dot(low, by_v[...], preferred_element_type=jnp.float32)
        for d in range(1, col_n):
            part_copy(i, d, c, (c + d) % col_n).start()
        product = lax.dot_general(
            pair_v[i], low, (((1,), (1,)), ((), ())), preferred_element_type=jnp.float32
        )
        gx_acc[...] = product if i == 0 else gx_acc[...] + product

    def gx1_copy(k, sender, target):
        j, b_to, g_to = target
        return remote(
            gx_acc.at[pl.ds(pl.multiple_of(j * piece, piece), piece)],
            gx_in.at[sender], gx1_s.at[k], gx1_r.at[k], {"grp": g_to, "row": 2 * a + b_to},
        )

    for k in range(1, team):
        gx1_copy(k, me_team, team_at(k)).start()
    gx_in[me_team] = gx_acc[pl.ds(pl.multiple_of(me_team * piece, piece), piece), :]

    def core_copy(i, owner):
        return remote(
            core_v.at[i], core.at[owner * half + i, 0], core_s.at[i], core_r.at[i],
            {"row": 2 * a + 1 - b},
        )

    core_writes = []
    for i in range(half):
        for d in range(1, col_n):
            sender = (c + col_n - d) % col_n
            part_copy(i, d, sender, sender).wait_recv()
        total = part_v[0, i]
        for j in range(1, col_n):
            total = total + part_v[j, i]
        core_v[i] = total
        core_copy(i, b).start()
        copy = pltpu.make_async_copy(core_v.at[i], core.at[b * half + i, 0], core_l.at[i])
        copy.start()
        core_writes.append(copy)
        product = lax.dot_general(
            proj_v[i], total.astype(jnp.bfloat16), (((0,), (0,)), ((), ())),
            preferred_element_type=jnp.float32,
        )
        gy_acc[...] = product if i == 0 else gy_acc[...] + product

    def gy_rows(b_to):
        return gy_acc.at[pl.ds(pl.multiple_of((2 * a + b_to) * part_y, part_y), part_y)]

    def gy_copy(k, sender, target):
        j, b_to, g_to = target
        return remote(
            gy_rows(b_to), gy_in.at[sender], gy_s.at[k], gy_r.at[k],
            {"grp": g_to, "row": 2 * a + b_to},
        )

    for k in range(1, team):
        gy_copy(k, me_team, team_at(k)).start()
    gy_in[me_team] = gy_acc[pl.ds(pl.multiple_of(r * part_y, part_y), part_y), :]

    for k in range(1, team):
        other = team_at(team - k)
        gx1_copy(k, other[0], other).wait_recv()
    total = gx_in[0]
    for j in range(1, team):
        total = total + gx_in[j]
    gx_piece[...] = total * scale_x

    def gx2_copy(k, sender, target):
        j, c_to, g_to = target
        return remote(
            gx_piece, gx_all.at[sender], gx2_s.at[k], gx2_r.at[k], {"grp": g_to, "col": c_to}
        )

    for k in range(1, ring):
        gx2_copy(k, me_ring, ring_at(k)).start()
    gx_all[me_ring] = gx_piece[...]

    for k in range(1, team):
        other = team_at(team - k)
        gy_copy(k, other[0], other).wait_recv()
    total = gy_in[0]
    for j in range(1, team):
        total = total + gy_in[j]
    gy_out[...] = total * scale_y
    gy_write = pltpu.make_async_copy(gy_out, gram_y, fin_sem.at[0])
    gy_write.start()

    for k in range(1, ring):
        other = ring_at(ring - k)
        gx2_copy(k, other[0], other).wait_recv()
    for e in range(grp_n):
        total = gx_all[e]
        for j in range(1, col_n):
            total = total + gx_all[j * grp_n + e]
        gx_out[e * piece : (e + 1) * piece, :] = total
    gx_write = pltpu.make_async_copy(gx_out, gram_x, fin_sem.at[1])
    gx_write.start()

    for i in range(half):
        core_copy(i, 1 - b).wait_recv()
        core_copy(i, b).wait_send()
        core_writes[i].wait()
        pair_copy(i, b).wait_send()
        for d in range(1, pairs):
            q_copy(i, d, a, (a + d) % pairs).wait_send()
        for d in range(1, col_n):
            part_copy(i, d, c, (c + d) % col_n).wait_send()
    for k in range(1, team):
        gx1_copy(k, me_team, team_at(k)).wait_send()
        gy_copy(k, me_team, team_at(k)).wait_send()
    for k in range(1, ring):
        gx2_copy(k, me_ring, ring_at(k)).wait_send()
    for k, (axis, at, n, out, into, send, recv) in enumerate(sides):

        @pl.when(at < n - 1)
        def _():
            halo(axis, at, out, into, send, recv, True, k == 0).wait_send()

        @pl.when(at > 0)
        def _():
            halo(axis, at, out, into, send, recv, False, k == 0).wait_send()

    for copy in writes:
        copy.wait()
    gy_write.wait()
    gx_write.wait()


def on_device(field, previous, kappa, rates, speeds, basis_x, basis_y):
    species, depth, width_x, width_y = field.shape
    rank = basis_x.shape[1]
    row_n = lax.axis_size("row")
    col_n = lax.axis_size("col")
    grp_n = lax.axis_size("grp")
    part_y = width_y // row_n
    grid_x = width_x * row_n
    grid_y = width_y * col_n
    grid_z = depth * grp_n
    scale_x = math.sqrt(grid_x) / (species * grid_z * grid_y)
    scale_y = math.sqrt(grid_y) / (species * grid_z * rank)
    half = species // 2
    pairs = row_n // 2
    piece = width_x // grp_n
    team = 2 * grp_n
    ring = grp_n * col_n
    f32, bf16 = jnp.float32, jnp.bfloat16
    dma = pltpu.SemaphoreType.DMA
    hbm = pl.BlockSpec(memory_space=pl.ANY)
    smem = pl.BlockSpec(memory_space=pltpu.SMEM)
    return pl.pallas_call(
        functools.partial(kernel, grp_n, row_n, col_n, scale_x, scale_y),
        out_shape=(
            jax.ShapeDtypeStruct(field.shape, f32),
            jax.ShapeDtypeStruct((species, depth, rank, rank), f32),
            jax.ShapeDtypeStruct((width_x, rank), f32),
            jax.ShapeDtypeStruct((part_y, rank), f32),
        ),
        in_specs=[hbm, hbm, hbm, smem, smem, hbm, hbm],
        out_specs=[hbm] * 4,
        scratch_shapes=[
            pltpu.VMEM((species, width_x, width_y), f32),
            pltpu.VMEM((width_x, width_y), f32),
            pltpu.VMEM((2 * width_x, rank), bf16),
            pltpu.VMEM((width_y, rank), bf16),
            pltpu.VMEM((half, 2 * width_x, width_y), bf16),
            pltpu.VMEM((pairs, half, rank, width_y), bf16),
            pltpu.VMEM((half, rank, width_y), bf16),
            pltpu.VMEM((col_n, half, rank, rank), f32),
            pltpu.VMEM((half, rank, rank), f32),
            pltpu.VMEM((2 * width_x, rank), f32),
            pltpu.VMEM((team, piece, rank), f32),
            pltpu.VMEM((piece, rank), f32),
            pltpu.VMEM((ring, piece, rank), f32),
            pltpu.VMEM((width_y, rank), f32),
            pltpu.VMEM((team, part_y, rank), f32),
            pltpu.VMEM((width_x, rank), f32),
            pltpu.VMEM((part_y, rank), f32),
            pltpu.VMEM((species, width_x, width_y), bf16),
            pltpu.VMEM((2, species, width_x, width_y), bf16),
            pltpu.VMEM((2, species, width_y), f32),
            pltpu.VMEM((2, species, width_y), f32),
            pltpu.VMEM((2, width_x, 128), f32),
            pltpu.VMEM((2, width_x, 128), f32),
            pltpu.VMEM((species, width_x, width_y), f32),
            dma((4,)), dma((half,)), dma((half,)), dma((half,)),
            dma((pairs, half)), dma((pairs, half)), dma((col_n, half)), dma((col_n, half)),
            dma((half,)), dma((half,)), dma((half,)),
            dma((team,)), dma((team,)), dma((ring,)), dma((ring,)), dma((team,)), dma((team,)),
            dma((2,)), dma((2,)), dma((2,)), dma((2,)), dma((2,)), dma((2,)),
            dma((species,)), dma((2,)),
        ],
        compiler_params=pltpu.CompilerParams(
            collective_id=0, has_side_effects=True, vmem_limit_bytes=40 * 1024 * 1024
        ),
    )(field, previous, kappa, rates, speeds, basis_x, basis_y)


def solution(mesh):
    return jax.shard_map(
        on_device,
        mesh=mesh,
        in_specs=(
            P(None, "grp", "row", "col"),
            P(None, "grp", "row", "col"),
            P("grp", "row", "col"),
            P(),
            P(),
            P(),
            P(),
        ),
        out_specs=(
            P(None, "grp", "row", "col"),
            P(None, "grp", None, None),
            P("row", None),
            P(("col", "row"), None),
        ),
        check_vma=False,
    )
```

time: 180 us -> 54.5 us (0.30)
  waiting for transfers between devices: 93.9 us -> 0 us
  Pallas kernels: 0 us -> 43.7 us
  starting transfers between devices: 22.3 us -> 0 us
  between operations: 15.7 us -> 0.65 us
  local copies, waits for them, and re-layouts: 21.9 us -> 9.89 us
  blocking collectives: 11.1 us -> 0 us
  other arithmetic: 10.5 us -> 0 us
  matrix products: 3.78 us -> 0 us
    psum x2 -> x0, waiting for transfers between devices: 72.5 us -> none  [the longest x1 40.4 us: on_device(): gram_x = lax.psum(local_x, ('grp', 'col'))]
    pallas_call x0 -> x1, Pallas kernels: none -> 43.7 us  [on_device(): pl.pallas_call(functools.partial(kernel, grp_n, row_n, col_n, scale_x, sc...]
    all_to_all x1 -> x0, waiting for transfers between devices: 19.6 us -> none  [on_device(): lax.all_to_all(previous, 'row', split_axis=3, concat_axis=2, tiled=True)]
    ppermute x6 -> x0, starting transfers between devices: 16.5 us -> none  [the longest x3 12.6 us: padded_2(): before = lax.ppermute(last, axis, up)]
    psum x1 -> x0, blocking collectives: 11.1 us -> none  [on_device(): gram_y = lax.psum(local_y, 'grp')]
    sub x1 -> x0, other arithmetic: 8.32 us -> none  [on_device(): field + kappa[None] * rates[:, None, None, None] * laplace - 0.5 * transport]
    all_to_all x1 -> x0, starting transfers between devices: 5.7 us -> none  [on_device(): lax.all_to_all(previous, 'row', split_axis=3, concat_axis=2, tiled=True)]
    slice x3 -> x0, local copies, waits for them, and re-layouts: 4.73 us -> none  [the longest x2 2.37 us: padded_2(): last = lax.slice_in_dim(value, length - width, length, axis=dim)]
  transfers between devices with their start and end apart: 10 -> 0, of which waited for: 5 -> 0; matrix products, arithmetic and copies ran while one was open for 17% -> 0% of each run, Pallas kernels for 0% -> 0%
where the time goes in v1:
time: 54.5 us; the launch traced here: 54.2 us
  Pallas kernels  43.7 us (80%)
  local copies, waits for them, and re-layouts  9.89 us (18%)
  between operations  0.65 us (1%)
    pallas_call x1, Pallas kernels, on_device(): pl.pallas_call(functools.partial(kernel, grp_n, row_n, col_n, scale_x, sc...  43.7 us
    unnamed x17, local copies, waits for them, and re-layouts  9.89 us

profile of v1, /device:TPU:0, one launch (start us, length us, event | category | flops | bytes accessed | tf_op | source)
XLA Modules:
  0.0 54.2 jit_solution(13759201622408304724)
XLA Ops:
  0.6 0.8 %copy.11.speeds = f32[8,3]{1,0:T(8,128)S(1)} copy(f32[8,3]{0,1:T(4,128)} %param.11) | data formatting | bytes 192 | tf_op args[4]
  1.4 0.0 copy-start
  1.4 1.4 %copy-done = f32[8,1,128,384]{3,2,1,0:T(8,128)S(1)} copy-done((f32[8,1,128,384]{3,2,1,0:T(8,128)S(1)}, f32[8,1,128,384]{3,2,1,0:T(8,128)}, u32[]{:S(2)}) %copy-start) | copy-done | bytes 1572888
  2.8 0.0 copy-start.1
  2.8 1.1 %copy-done.1 = bf16[8,1,128,384]{3,2,1,0:T(8,128)(2,1)S(1)} copy-done((bf16[8,1,128,384]{3,2,1,0:T(8,128)(2,1)S(1)}, bf16[8,1,128,384]{3,2,1,0:T(8,128)(2,1)}, u32[]{:S(2)}) %copy-start.1) | copy-done | bytes 786456
  3.9 0.0 copy-start.2
  3.9 0.9 %copy-done.2 = f32[1,128,384]{2,1,0:T(8,128)S(1)} copy-done((f32[1,128,384]{2,1,0:T(8,128)S(1)}, f32[1,128,384]{2,1,0:T(8,128)}, u32[]{:S(2)}) %copy-start.2) | copy-done | bytes 196632
  4.9 0.0 copy-start.3
  4.9 0.9 %copy-done.3 = bf16[768,128]{1,0:T(8,128)(2,1)S(1)} copy-done((bf16[768,128]{1,0:T(8,128)(2,1)S(1)}, bf16[768,128]{1,0:T(8,128)(2,1)}, u32[]{:S(2)}) %copy-start.3) | copy-done | bytes 196632
  5.8 0.0 copy-start.4
  5.8 0.9 %copy-done.4 = bf16[512,128]{1,0:T(8,128)(2,1)S(1)} copy-done((bf16[512,128]{1,0:T(8,128)(2,1)S(1)}, bf16[512,128]{1,0:T(8,128)(2,1)}, u32[]{:S(2)}) %copy-start.4) | copy-done | bytes 131096
  6.7 0.0 copy-start.5
  6.7 0.7 %copy-done.5 = f32[8]{0:T(128)S(1)} copy-done((f32[8]{0:T(128)S(1)}, f32[8]{0:T(128)}, u32[]{:S(2)}) %copy-start.5) | copy-done | bytes 56
  7.3 43.7 %shard_map.102 = (f32[8,1,128,384]{3,2,1,0:T(8,128)S(1)}, f32[8,1,128,128]{3,2,1,0:T(8,128)S(1)}, f32[128,128]{1,0:T(8,128)S(1)}, f32[96,128]{1,0:T(8,128)S(1)}) custom-call(f32[8,1,128,384]{3,2,1,0:T(8,128)S(1)} %copy-done, bf16[8,1,128,384]{3,2,1,0:T(8,128)(2,1)S(1)} %copy-done.1, f32[1,128,384]{2,1,0:T(8,128)S(1)} %copy-done.2, f32[8]{0:T(128)S(1)} %copy-done.5, ...), custom_call_target="tpu_custom_call" | custom-call | tf_op jit(solution)/shard_map/pallas_call | solution.py:398
  51.1 1.1 %copy.16 = f32[8,1,128,384]{3,2,1,0:T(8,128)} copy(f32[8,1,128,384]{3,2,1,0:T(8,128)S(1)} %get-tuple-element.8) | data formatting | bytes 3145728
  52.2 0.8 %copy.17 = f32[8,1,128,128]{3,2,1,0:T(8,128)} copy(f32[8,1,128,128]{3,2,1,0:T(8,128)S(1)} %get-tuple-element.9) | data formatting | bytes 1048576
  53.0 0.6 %copy.18 = f32[128,128]{1,0:T(8,128)} copy(f32[128,128]{1,0:T(8,128)S(1)} %get-tuple-element.10) | data formatting | bytes 131072
  53.6 0.6 %copy.19 = f32[96,128]{1,0:T(8,128)} copy(f32[96,128]{1,0:T(8,128)S(1)} %get-tuple-element.11) | data formatting | bytes 98304
Async XLA Ops:
  1.4 1.4 %copy-start = (f32[8,1,128,384]{3,2,1,0:T(8,128)S(1)}, f32[8,1,128,384]{3,2,1,0:T(8,128)}, u32[]{:S(2)}) copy-start(f32[8,1,128,384]{3,2,1,0:T(8,128)} %field.1) | copy-start | bytes 4718596
  2.8 1.1 %copy-start.1 = (bf16[8,1,128,384]{3,2,1,0:T(8,128)(2,1)S(1)}, bf16[8,1,128,384]{3,2,1,0:T(8,128)(2,1)}, u32[]{:S(2)}) copy-start(bf16[8,1,128,384]{3,2,1,0:T(8,128)(2,1)} %prev.1) | copy-start | bytes 2359300
  3.9 0.9 %copy-start.2 = (f32[1,128,384]{2,1,0:T(8,128)S(1)}, f32[1,128,384]{2,1,0:T(8,128)}, u32[]{:S(2)}) copy-start(f32[1,128,384]{2,1,0:T(8,128)} %kappa.1) | copy-start | bytes 589828
  4.9 0.9 %copy-start.3 = (bf16[768,128]{1,0:T(8,128)(2,1)S(1)}, bf16[768,128]{1,0:T(8,128)(2,1)}, u32[]{:S(2)}) copy-start(bf16[768,128]{1,0:T(8,128)(2,1)} %basis_y.1) | copy-start | bytes 589828
  5.8 0.9 %copy-start.4 = (bf16[512,128]{1,0:T(8,128)(2,1)S(1)}, bf16[512,128]{1,0:T(8,128)(2,1)}, u32[]{:S(2)}) copy-start(bf16[512,128]{1,0:T(8,128)(2,1)} %basis_x.1) | copy-start | bytes 393220
  6.7 0.7 %copy-start.5 = (f32[8]{0:T(128)S(1)}, f32[8]{0:T(128)}, u32[]{:S(2)}) copy-start(f32[8]{0:T(128)} %rates.1) | copy-start | bytes 100

commit v2 on v1

--- a/solution.py
+++ b/solution.py
@@ -20,6 +20,18 @@
         device_id=target,
         device_id_type=MESH,
     )
+
+
+def coded(value):
+    square = value * value
+    fourth = square * square
+    return jnp.where(value < 0.0, -fourth, fourth).astype(jnp.bfloat16)
+
+
+def decoded(code):
+    wide = code.astype(jnp.float32)
+    root = jnp.sqrt(jnp.sqrt(jnp.abs(wide)))
+    return jnp.where(wide < 0.0, -root, root)
 
 
 def kernel(
@@ -174,9 +186,12 @@
     for i in range(half):
         mine[i].wait()
         pair_copy(i, 1 - b).wait_recv()
-        q_v[a, i] = lax.dot_general(
-            bx_v[...], pair_v[i], (((0,), (0,)), ((), ())), preferred_element_type=jnp.float32
-        ).astype(jnp.bfloat16)
+        q_v[a, i] = coded(
+            lax.dot_general(
+                bx_v[...], pair_v[i], (((0,), (0,)), ((), ())),
+                preferred_element_type=jnp.float32,
+            )
+        )
         for d in range(1, pairs):
             q_copy(i, d, a, (a + d) % pairs).start()
 
@@ -222,9 +237,9 @@
         )
         laplace = z_next + z_prev + x_next + x_prev + y_next + y_prev - 6.0 * u
         transport = (
-            speeds[s, 0] * (z_next - z_prev)
-            + speeds[s, 1] * (x_next - x_prev)
-            + speeds[s, 2] * (y_next - y_prev)
+            speeds[0, s] * (z_next - z_prev)
+            + speeds[1, s] * (x_next - x_prev)
+            + speeds[2, s] * (y_next - y_prev)
         )
         adv_v[s] = u + kappa_v[...] * rates[s] * laplace - 0.5 * transport
         copy = pltpu.make_async_copy(adv_v.at[s], advanced.at[s, 0], out_sem.at[s])
@@ -242,9 +257,9 @@
         for d in range(1, pairs):
             sender = (a + pairs - d) % pairs
             q_copy(i, d, sender, sender).wait_recv()
-        total = q_v[0, i].astype(jnp.float32)
+        total = decoded(q_v[0, i])
         for j in range(1, pairs):
-            total = total + q_v[j, i].astype(jnp.float32)
+            total = total + decoded(q_v[j, i])
         low = total.astype(jnp.bfloat16)
         proj_v[i] = low
         part_v[c, i] = jnp.dot(low, by_v[...], preferred_element_type=jnp.float32)
@@ -438,9 +453,9 @@
             dma((species,)), dma((2,)),
         ],
         compiler_params=pltpu.CompilerParams(
-            collective_id=0, has_side_effects=True, vmem_limit_bytes=40 * 1024 * 1024
-        ),
-    )(field, previous, kappa, rates, speeds, basis_x, basis_y)
+            collective_id=0, has_side_effects=True, vmem_limit_bytes=60 * 1024 * 1024
+        ),
+    )(field, previous, kappa, rates, speeds.T, basis_x, basis_y)
 
 
 def solution(mesh):

time: 54.5 us -> 48.8 us (0.90)
  local copies, waits for them, and re-layouts: 9.89 us -> 4.78 us
    unnamed x17 -> x10, local copies, waits for them, and re-layouts: 9.89 us -> 4.78 us
where the time goes in v2:
time: 48.8 us; the launch traced here: 48.6 us
  Pallas kernels  43.2 us (89%)
  local copies, waits for them, and re-layouts  4.78 us (10%)
  between operations  0.67 us (1%)
    pallas_call x1, Pallas kernels, on_device(): pl.pallas_call(functools.partial(kernel, grp_n, row_n, col_n, scale_x, sc...  43.2 us
    unnamed x10, local copies, waits for them, and re-layouts  4.78 us

profile of v2, /device:TPU:0, one launch (start us, length us, event | category | flops | bytes accessed | tf_op | source)
XLA Modules:
  0.0 48.6 jit_solution(10457737677295604865)
XLA Ops:
  0.6 43.2 %shard_map.102 = (f32[8,1,128,384]{3,2,1,0:T(8,128)}, f32[8,1,128,128]{3,2,1,0:T(8,128)}, f32[128,128]{1,0:T(8,128)}, f32[96,128]{1,0:T(8,128)}) custom-call(f32[8,1,128,384]{3,2,1,0:T(8,128)} %field.1, bf16[8,1,128,384]{3,2,1,0:T(8,128)(2,1)} %prev.1, f32[1,128,384]{2,1,0:T(8,128)} %kappa.1, f32[8]{0:T(128)} %rates.1, f32[3,8]{1,0:T(4,128)} %bitcast.1, ...), custom_call_target="tpu_custom_call" | custom-call | tf_op jit(solution)/shard_map/pallas_call | solution.py:413
  43.8 0.0 copy-start
  43.8 0.0 copy-start.1
  43.8 0.0 copy-start.2
  43.8 2.7 %copy.15 = f32[8,1,128,384]{3,2,1,0:T(8,128)} copy(f32[8,1,128,384]{3,2,1,0:T(8,128)} %get-tuple-element.8) | data formatting | bytes 3145728
  46.6 0.0 copy-done
  46.6 0.8 %copy.16 = f32[8,1,128,128]{3,2,1,0:T(8,128)} copy(f32[8,1,128,128]{3,2,1,0:T(8,128)S(1)} %copy-done) | data formatting | bytes 1048576
  47.4 0.0 copy-done.1
  47.4 0.6 %copy.17 = f32[128,128]{1,0:T(8,128)} copy(f32[128,128]{1,0:T(8,128)S(1)} %copy-done.1) | data formatting | bytes 131072
  48.0 0.0 copy-done.2
  48.0 0.6 %copy.18 = f32[96,128]{1,0:T(8,128)} copy(f32[96,128]{1,0:T(8,128)S(1)} %copy-done.2) | data formatting | bytes 98304
Async XLA Ops:
  43.8 2.8 %copy-start = (f32[8,1,128,128]{3,2,1,0:T(8,128)S(1)}, f32[8,1,128,128]{3,2,1,0:T(8,128)}, u32[]{:S(2)}) copy-start(f32[8,1,128,128]{3,2,1,0:T(8,128)} %get-tuple-element.9) | copy-start | bytes 1572868
  43.8 3.5 %copy-start.1 = (f32[128,128]{1,0:T(8,128)S(1)}, f32[128,128]{1,0:T(8,128)}, u32[]{:S(2)}) copy-start(f32[128,128]{1,0:T(8,128)} %get-tuple-element.10) | copy-start | bytes 196612
  43.8 4.2 %copy-start.2 = (f32[96,128]{1,0:T(8,128)S(1)}, f32[96,128]{1,0:T(8,128)}, u32[]{:S(2)}) copy-start(f32[96,128]{1,0:T(8,128)} %get-tuple-element.11) | copy-start | bytes 147460

commit v3 on v2

--- a/solution.py
+++ b/solution.py
@@ -34,12 +34,23 @@
     return jnp.where(wide < 0.0, -root, root)
 
 
+def squared(value):
+    square = value * value
+    return jnp.where(value < 0.0, -square, square).astype(jnp.bfloat16)
+
+
+def rooted(code):
+    wide = code.astype(jnp.float32)
+    root = jnp.sqrt(jnp.abs(wide))
+    return jnp.where(wide < 0.0, -root, root)
+
+
 def kernel(
     grp_n, row_n, col_n, scale_x, scale_y,
     field, prev, kappa, rates, speeds, basis_x, basis_y,
     advanced, core, gram_x, gram_y,
-    field_v, kappa_v, bx_v, by_v, pair_v, q_v, proj_v, part_v, core_v,
-    gx_acc, gx_in, gx_piece, gx_all, gy_acc, gy_in, gx_out, gy_out,
+    field_v, kappa_v, bx_v, by_v, pair_v, q_v, proj_v, part_v, core_v, core_out, core_in,
+    gx_acc, gx_code, gx_in, gx_piece, gx_all, gy_acc, gy_code, gy_in, gx_out, gy_out,
     z_out, z_in, x_out, x_in, y_out, y_in, adv_v,
     in_sem, own_sem, pair_s, pair_r, q_s, q_r, part_s, part_r, core_s, core_r, core_l,
     gx1_s, gx1_r, gx2_s, gx2_r, gy_s, gy_r, z_s, z_r, x_s, x_r, y_s, y_r, out_sem, fin_sem,
@@ -252,6 +263,32 @@
             {"col": target},
         )
 
+    def core_copy(i):
+        return remote(
+            core_out.at[i], core_in.at[i], core_s.at[i], core_r.at[i], {"row": 2 * a + 1 - b}
+        )
+
+    def core_write(i, owner, at):
+        return pltpu.make_async_copy(
+            core_v.at[at, i], core.at[owner * half + i, 0], core_l.at[at, i]
+        )
+
+    def finish_core(i):
+        for d in range(1, col_n):
+            sender = (c + col_n - d) % col_n
+            part_copy(i, d, sender, sender).wait_recv()
+        total = part_v[0, i]
+        for j in range(1, col_n):
+            total = total + part_v[j, i]
+        code = coded(total)
+        core_out[i] = code
+        core_copy(i).start()
+        product = lax.dot_general(
+            proj_v[i], total.astype(jnp.bfloat16), (((0,), (0,)), ((), ())),
+            preferred_element_type=jnp.float32,
+        )
+        gy_acc[...] = product if i == 0 else gy_acc[...] + product
+
     loads[3].wait()
     for i in range(half):
         for d in range(1, pairs):
@@ -269,45 +306,25 @@
             pair_v[i], low, (((1,), (1,)), ((), ())), preferred_element_type=jnp.float32
         )
         gx_acc[...] = product if i == 0 else gx_acc[...] + product
+        if 0 < i < half - 1:
+            finish_core(i - 1)
 
     def gx1_copy(k, sender, target):
         j, b_to, g_to = target
         return remote(
-            gx_acc.at[pl.ds(pl.multiple_of(j * piece, piece), piece)],
+            gx_code.at[pl.ds(pl.multiple_of(j * piece, piece), piece)],
             gx_in.at[sender], gx1_s.at[k], gx1_r.at[k], {"grp": g_to, "row": 2 * a + b_to},
         )
 
+    gx_code[...] = squared(gx_acc[...])
     for k in range(1, team):
         gx1_copy(k, me_team, team_at(k)).start()
-    gx_in[me_team] = gx_acc[pl.ds(pl.multiple_of(me_team * piece, piece), piece), :]
-
-    def core_copy(i, owner):
-        return remote(
-            core_v.at[i], core.at[owner * half + i, 0], core_s.at[i], core_r.at[i],
-            {"row": 2 * a + 1 - b},
-        )
-
-    core_writes = []
-    for i in range(half):
-        for d in range(1, col_n):
-            sender = (c + col_n - d) % col_n
-            part_copy(i, d, sender, sender).wait_recv()
-        total = part_v[0, i]
-        for j in range(1, col_n):
-            total = total + part_v[j, i]
-        core_v[i] = total
-        core_copy(i, b).start()
-        copy = pltpu.make_async_copy(core_v.at[i], core.at[b * half + i, 0], core_l.at[i])
-        copy.start()
-        core_writes.append(copy)
-        product = lax.dot_general(
-            proj_v[i], total.astype(jnp.bfloat16), (((0,), (0,)), ((), ())),
-            preferred_element_type=jnp.float32,
-        )
-        gy_acc[...] = product if i == 0 else gy_acc[...] + product
+    gx_in[me_team] = gx_code[pl.ds(pl.multiple_of(me_team * piece, piece), piece), :]
+    for i in range(max(half - 2, 0), half):
+        finish_core(i)
 
     def gy_rows(b_to):
-        return gy_acc.at[pl.ds(pl.multiple_of((2 * a + b_to) * part_y, part_y), part_y)]
+        return gy_code.at[pl.ds(pl.multiple_of((2 * a + b_to) * part_y, part_y), part_y)]
 
     def gy_copy(k, sender, target):
         j, b_to, g_to = target
@@ -316,16 +333,17 @@
             {"grp": g_to, "row": 2 * a + b_to},
         )
 
+    gy_code[...] = squared(gy_acc[...])
     for k in range(1, team):
         gy_copy(k, me_team, team_at(k)).start()
-    gy_in[me_team] = gy_acc[pl.ds(pl.multiple_of(r * part_y, part_y), part_y), :]
+    gy_in[me_team] = gy_code[pl.ds(pl.multiple_of(r * part_y, part_y), part_y), :]
 
     for k in range(1, team):
         other = team_at(team - k)
         gx1_copy(k, other[0], other).wait_recv()
-    total = gx_in[0]
+    total = rooted(gx_in[0])
     for j in range(1, team):
-        total = total + gx_in[j]
+        total = total + rooted(gx_in[j])
     gx_piece[...] = total * scale_x
 
     def gx2_copy(k, sender, target):
@@ -338,12 +356,19 @@
         gx2_copy(k, me_ring, ring_at(k)).start()
     gx_all[me_ring] = gx_piece[...]
 
+    for i in range(half):
+        core_v[0, i] = decoded(core_out[i])
+        core_write(i, b, 0).start()
+        core_copy(i).wait_recv()
+        core_v[1, i] = decoded(core_in[i])
+        core_write(i, 1 - b, 1).start()
+
     for k in range(1, team):
         other = team_at(team - k)
         gy_copy(k, other[0], other).wait_recv()
-    total = gy_in[0]
+    total = rooted(gy_in[0])
     for j in range(1, team):
-        total = total + gy_in[j]
+        total = total + rooted(gy_in[j])
     gy_out[...] = total * scale_y
     gy_write = pltpu.make_async_copy(gy_out, gram_y, fin_sem.at[0])
     gy_write.start()
@@ -360,9 +385,9 @@
     gx_write.start()
 
     for i in range(half):
-        core_copy(i, 1 - b).wait_recv()
-        core_copy(i, b).wait_send()
-        core_writes[i].wait()
+        core_copy(i).wait_send()
+        core_write(i, b, 0).wait()
+        core_write(i, 1 - b, 1).wait()
         pair_copy(i, b).wait_send()
         for d in range(1, pairs):
             q_copy(i, d, a, (a + d) % pairs).wait_send()
@@ -429,13 +454,17 @@
             pltpu.VMEM((pairs, half, rank, width_y), bf16),
             pltpu.VMEM((half, rank, width_y), bf16),
             pltpu.VMEM((col_n, half, rank, rank), f32),
-            pltpu.VMEM((half, rank, rank), f32),
+            pltpu.VMEM((2, half, rank, rank), f32),
+            pltpu.VMEM((half, rank, rank), bf16),
+            pltpu.VMEM((half, rank, rank), bf16),
             pltpu.VMEM((2 * width_x, rank), f32),
-            pltpu.VMEM((team, piece, rank), f32),
+            pltpu.VMEM((2 * width_x, rank), bf16),
+            pltpu.VMEM((team, piece, rank), bf16),
             pltpu.VMEM((piece, rank), f32),
             pltpu.VMEM((ring, piece, rank), f32),
             pltpu.VMEM((width_y, rank), f32),
-            pltpu.VMEM((team, part_y, rank), f32),
+            pltpu.VMEM((width_y, rank), bf16),
+            pltpu.VMEM((team, part_y, rank), bf16),
             pltpu.VMEM((width_x, rank), f32),
             pltpu.VMEM((part_y, rank), f32),
             pltpu.VMEM((species, width_x, width_y), bf16),
@@ -447,7 +476,7 @@
             pltpu.VMEM((species, width_x, width_y), f32),
             dma((4,)), dma((half,)), dma((half,)), dma((half,)),
             dma((pairs, half)), dma((pairs, half)), dma((col_n, half)), dma((col_n, half)),
-            dma((half,)), dma((half,)), dma((half,)),
+            dma((half,)), dma((half,)), dma((2, half)),
             dma((team,)), dma((team,)), dma((ring,)), dma((ring,)), dma((team,)), dma((team,)),
             dma((2,)), dma((2,)), dma((2,)), dma((2,)), dma((2,)), dma((2,)),
             dma((species,)), dma((2,)),

time: 48.8 us -> 44.9 us (0.920)
  Pallas kernels: 43.2 us -> 39.3 us
    pallas_call x1, Pallas kernels: 43.2 us -> 39.3 us  [on_device(): pl.pallas_call(functools.partial(kernel, grp_n, row_n, col_n, scale_x, sc...]
where the time goes in v3:
time: 44.9 us; the launch traced here: 44.8 us
  Pallas kernels  39.3 us (88%)
  local copies, waits for them, and re-layouts  4.78 us (11%)
  between operations  0.67 us (1%)
    pallas_call x1, Pallas kernels, on_device(): pl.pallas_call(functools.partial(kernel, grp_n, row_n, col_n, scale_x, sc...  39.3 us
    unnamed x10, local copies, waits for them, and re-layouts  4.78 us

profile of v3, /device:TPU:0, one launch (start us, length us, event | category | flops | bytes accessed | tf_op | source)
XLA Modules:
  0.0 44.8 jit_solution(17112907056991750702)
XLA Ops:
  0.6 39.3 %shard_map.102 = (f32[8,1,128,384]{3,2,1,0:T(8,128)}, f32[8,1,128,128]{3,2,1,0:T(8,128)}, f32[128,128]{1,0:T(8,128)}, f32[96,128]{1,0:T(8,128)}) custom-call(f32[8,1,128,384]{3,2,1,0:T(8,128)} %field.1, bf16[8,1,128,384]{3,2,1,0:T(8,128)(2,1)} %prev.1, f32[1,128,384]{2,1,0:T(8,128)} %kappa.1, f32[8]{0:T(128)} %rates.1, f32[3,8]{1,0:T(4,128)} %bitcast.1, ...), custom_call_target="tpu_custom_call" | custom-call | tf_op jit(solution)/shard_map/pallas_call | solution.py:438
  40.0 0.0 copy-start
  40.0 0.0 copy-start.1
  40.0 0.0 copy-start.2
  40.0 2.7 %copy.15 = f32[8,1,128,384]{3,2,1,0:T(8,128)} copy(f32[8,1,128,384]{3,2,1,0:T(8,128)} %get-tuple-element.8) | data formatting | bytes 3145728
  42.7 0.0 copy-done
  42.7 0.8 %copy.16 = f32[8,1,128,128]{3,2,1,0:T(8,128)} copy(f32[8,1,128,128]{3,2,1,0:T(8,128)S(1)} %copy-done) | data formatting | bytes 1048576
  43.5 0.0 copy-done.1
  43.5 0.6 %copy.17 = f32[128,128]{1,0:T(8,128)} copy(f32[128,128]{1,0:T(8,128)S(1)} %copy-done.1) | data formatting | bytes 131072
  44.1 0.0 copy-done.2
  44.1 0.6 %copy.18 = f32[96,128]{1,0:T(8,128)} copy(f32[96,128]{1,0:T(8,128)S(1)} %copy-done.2) | data formatting | bytes 98304
Async XLA Ops:
  40.0 2.8 %copy-start = (f32[8,1,128,128]{3,2,1,0:T(8,128)S(1)}, f32[8,1,128,128]{3,2,1,0:T(8,128)}, u32[]{:S(2)}) copy-start(f32[8,1,128,128]{3,2,1,0:T(8,128)} %get-tuple-element.9) | copy-start | bytes 1572868
  40.0 3.5 %copy-start.1 = (f32[128,128]{1,0:T(8,128)S(1)}, f32[128,128]{1,0:T(8,128)}, u32[]{:S(2)}) copy-start(f32[128,128]{1,0:T(8,128)} %get-tuple-element.10) | copy-start | bytes 196612
  40.0 4.2 %copy-start.2 = (f32[96,128]{1,0:T(8,128)S(1)}, f32[96,128]{1,0:T(8,128)}, u32[]{:S(2)}) copy-start(f32[96,128]{1,0:T(8,128)} %get-tuple-element.11) | copy-start | bytes 147460
